TPU v7x, 512 devices: a whole 4x8x8 slice. The times are simulated.
512 devices in a mesh: sub: 64 (over y, x, core), grp: 8 (over z).
Axes of the slice: x: 4, y: 8, z: 8, core: 2. Of those that a mesh axis runs over, the one named last changes fastest.
Arguments:
- deflation: bfloat16 [64, 48, 40, 128], P('sub', 'grp'), may hold values from -0.59765625 to 0.59765625
- operator_tiles: bfloat16 [64, 48, 9, 128, 128], P('sub', 'grp'), may hold values from -0.1875 to 0.1875
- tile_columns: int32 [64, 48, 9], P('sub', 'grp'), may hold values from 0 to 95, as said below
- neighbours: int32 [64, 6], P('sub'), may hold values from -1 to 5, as said below
- send_blocks: int32 [64, 6, 8], P('sub'), may hold values from 0 to 47
- row_owner: int32 [64], replicated, may hold values from 0 to 63, each once
Outputs:
- coarse: float32 [64, 40, 280], P('sub', 'grp')
Inputs may be any that keep to these rules, and one draw needn't show every extreme that they name: Neighbour ranks list offset slots in increasing order, then -1; the graph is symmetric (j is a neighbour of i exactly when i is one of j), never names a subdomain outside 0 .. 63, offset +1 is always an edge where it exists, and subdomain 64 // 2 has all six neighbours. `tile_columns`: tile 0 of block row b names the subdomain's own block b; a value 48 + r * 8 + n names only a rank r below the subdomain's degree.
All inputs are finite; a program needn't handle non-finite values.
Results may differ from a plain program's by a relative error of at most 0.01.
Values may be sent and summed in bfloat16 or wider, within the bound.
A program may use at most 64 MiB of HBM per device.

v0:
```python
import jax
import jax.numpy as jnp
from jax import lax
from jax.sharding import PartitionSpec as P


def shifted(value, axis, steps):
    count = lax.axis_size(axis)
    leading, last = (max(0, -steps), min(count, count - steps))
    return lax.ppermute(value, axis, [(source, source + steps) for source in range(leading, last)])


def shards(deflation, operator_tiles, tile_columns, neighbours, send_blocks, row_owner):
    subdomain_panel = lax.all_gather(deflation[0], "grp", axis=0, tiled=True)
    block_count = subdomain_panel.shape[0]
    width = subdomain_panel.shape[1]
    lane_rows = subdomain_panel.shape[2]
    offsets = [1, 2, 3, -1, -2, -3]
    pieces = []
    for slot_pos, offset in enumerate(offsets):
        chosen = jnp.take(subdomain_panel, send_blocks[0, slot_pos], axis=0)
        pieces.append(shifted(chosen, "sub", -offset))
    received = jnp.stack(pieces, axis=0)
    rank_list = neighbours[0]
    ranked = jnp.take(received, jnp.clip(rank_list, 0, 5), axis=0)
    ranked = jnp.where((rank_list >= 0)[:, None, None, None], ranked, jnp.zeros_like(ranked))
    send_count = received.shape[1]
    columns_all = jnp.concatenate(
        [subdomain_panel, ranked.reshape(6 * send_count, width, lane_rows)], axis=0
    )
    own_columns = tile_columns[0]
    tile_panels = jnp.take(columns_all, own_columns, axis=0)
    products = jnp.einsum(
        "btkc,btrc->btkr", tile_panels, operator_tiles[0], preferred_element_type=jnp.float32
    )
    slot_of = jnp.where(own_columns < block_count, 0, 1 + (own_columns - block_count) // send_count)
    slot_total = 7
    picker = (slot_of[:, :, None] == jnp.arange(slot_total)[None, None, :]).astype(jnp.float32)
    image_blocks = jnp.einsum("bts,btkr->bskr", picker, products).astype(jnp.bfloat16)
    galerkin = jnp.einsum(
        "bar,bskr->ask", deflation[0], image_blocks, preferred_element_type=jnp.float32
    )
    galerkin = galerkin.reshape(width, slot_total * width)
    my_index = lax.axis_index("sub")
    count_sub = lax.axis_size("sub")
    target = row_owner[my_index]
    placed = jnp.where(jnp.arange(count_sub)[:, None, None] == target, galerkin[None], 0.0)
    placed = placed.reshape(count_sub * width, slot_total * width)
    summed = lax.psum_scatter(placed, ("sub", "grp"), scatter_dimension=0, tiled=True)
    return summed[None]


def solution(mesh):
    placed = (
        P("sub", "grp", None, None),
        P("sub", "grp", None, None, None),
        P("sub", "grp", None),
        P("sub", None),
        P("sub", None, None),
        P(),
    )
    return jax.shard_map(
        shards, mesh=mesh, in_specs=placed, out_specs=P("sub", "grp", None), check_vma=False
    )
```

profile of v0, /device:TPU:1, one launch (start us, length us, event | category | flops | bytes accessed | tf_op | source)
XLA Modules:
  0.0 372.3 jit_solution(12682578110151546582)
XLA Ops:
  6.5 0.9 compare_and_fusion.1
  7.4 27.0 %all-gather = bf16[1,48,40,128]{3,2,0,1:T(8,128)(2,1)S(1)} all-gather(bf16[1,6,40,128]{3,2,0,1:T(8,128)(2,1)} %bitcast.105), channel_id=2, replica_groups=mesh['sub'=64,'grp'=8] {'grp'}, dimensions={1}, use_global_device_ids=true | all-gather | bytes 552960 | tf_op jit(solution)/shard_map/all_gather | solution.py:14
  34.5 0.6 gather_fusion.2
  35.1 8.1 %collective-permute-start = (bf16[8,40,128]{2,1,0:T(8,128)(2,1)S(1)}, bf16[8,40,128]{2,1,0:T(8,128)(2,1)S(1)}, u32[]{:S(2)}, u32[]{:S(2)}) collective-permute-start(bf16[8,40,128]{2,1,0:T(8,128)(2,1)S(1)} %broadcast_select_fusion.5), channel_id=1, source_target_pairs={{8,0},{16,8},{24,16},{32,24},{40,32},{48,40},{56,48},{64,56},{72,6... | collective-permute-start | bytes 245768 | tf_op jit(solution)/shard_map/ppermute | solution.py:10
  43.3 0.6 gather_fusion.3
  44.0 1.3 collective-permute-start.1
  45.3 0.6 gather_fusion.4
  45.9 1.3 collective-permute-start.2
  47.2 0.6 gather_fusion.5
  47.9 3.6 collective-permute-start.3
  51.6 0.6 gather_fusion.6
  52.1 0.7 broadcast_select_fusion.1
  52.8 4.9 %collective-permute-start.4 = (bf16[8,40,128]{2,1,0:T(8,128)(2,1)}, bf16[8,40,128]{2,1,0:T(8,128)(2,1)}, u32[]{:S(2)}, u32[]{:S(2)}) collective-permute-start(bf16[8,40,128]{2,1,0:T(8,128)(2,1)} %broadcast_select_fusion.1), channel_id=1, source_target_pairs={{0,16},{8,24},{16,32},{24,40},{32,48},{40,56},{48,64},{56,72},{64,... | collective-permute-start | bytes 245768 | tf_op jit(solution)/shard_map/ppermute | solution.py:10
  57.7 0.7 fusion.25
  58.4 0.7 compare_bitcast_fusion
  59.1 0.7 compare_and_fusion.7
  59.7 0.7 fusion.24
  60.4 0.7 compare_and_fusion
  61.1 0.7 fusion.19
  61.8 0.6 gather_fusion.7
  62.8 1.2 dynamic_slice.3
  64.1 0.6 iota_compare_fusion.1
  65.0 4.0 %collective-permute-start.5 = (bf16[8,40,128]{2,1,0:T(8,128)(2,1)S(1)}, bf16[8,40,128]{2,1,0:T(8,128)(2,1)S(1)}, u32[]{:S(2)}, u32[]{:S(2)}) collective-permute-start(bf16[8,40,128]{2,1,0:T(8,128)(2,1)S(1)} %broadcast_select_fusion), channel_id=1, source_target_pairs={{0,24},{8,32},{16,40},{24,48},{32,56},{40,64},{48,72},{56,80},{64,... | collective-permute-start | bytes 245768 | tf_op jit(solution)/shard_map/ppermute | solution.py:10
  69.2 0.9 bitcast_dynamic-update-slice_fusion.1
  70.1 1.2 collective-permute-done.5
  71.3 0.6 gather_fusion
  72.2 1.5 gather_fusion.1
  73.7 2.3 fusion.2
  76.7 2.3 bitcast_select_fusion
  79.0 285.1 %all-reduce.3.cloned.1.call-done = f32[2560,280]{1,0:T(8,128)} async-done(((f32[2560,280]{1,0:T(8,128)}), f32[2560,280]{1,0:T(8,128)}) %all-reduce.3.cloned.1.call-update) | async-done | bytes 2867216
  364.2 0.7 dynamic-slice_bitcast_fusion
  364.9 0.6 copy.13
  (41 shorter events, 2.0 us)
Async XLA Ops:
  6.5 67.2 %copy-start = (bf16[1,6,9,128,128]{4,3,2,1,0:T(8,128)(2,1)S(1)}, bf16[1,6,9,128,128]{4,3,2,1,0:T(8,128)(2,1)}, u32[]{:S(2)}) copy-start(bf16[1,6,9,128,128]{4,3,2,1,0:T(8,128)(2,1)} %param.9) | copy-start | bytes 5308420
  6.5 357.6 %all-reduce.3.cloned.1.call-start = ((), (), s32[]{:S(2)}) async-start(), calls=%async_computation | async-start | bytes 7864320
  35.1 29.9 %collective-permute-start = (bf16[8,40,128]{2,1,0:T(8,128)(2,1)S(1)}, bf16[8,40,128]{2,1,0:T(8,128)(2,1)S(1)}, u32[]{:S(2)}, u32[]{:S(2)}) collective-permute-start(bf16[8,40,128]{2,1,0:T(8,128)(2,1)S(1)} %broadcast_select_fusion.5), channel_id=1, source_target_pairs={{8,0},{16,8},{24,16},{32,24},{40,32},{48,40},{56,48},{64,56},{72,6... | collective-permute-start | bytes 245768 | tf_op jit(solution)/shard_map/ppermute | solution.py:10
  44.0 25.1 %collective-permute-start.1 = (bf16[8,40,128]{2,1,0:T(8,128)(2,1)S(1)}, bf16[8,40,128]{2,1,0:T(8,128)(2,1)S(1)}, u32[]{:S(2)}, u32[]{:S(2)}) collective-permute-start(bf16[8,40,128]{2,1,0:T(8,128)(2,1)S(1)} %broadcast_select_fusion.4), channel_id=1, source_target_pairs={{16,0},{24,8},{32,16},{40,24},{48,32},{56,40},{64,48},{72,56},{80,... | collective-permute-start | bytes 245768 | tf_op jit(solution)/shard_map/ppermute | solution.py:10
  45.9 23.2 %collective-permute-start.2 = (bf16[8,40,128]{2,1,0:T(8,128)(2,1)S(1)}, bf16[8,40,128]{2,1,0:T(8,128)(2,1)S(1)}, u32[]{:S(2)}, u32[]{:S(2)}) collective-permute-start(bf16[8,40,128]{2,1,0:T(8,128)(2,1)S(1)} %broadcast_select_fusion.3), channel_id=1, source_target_pairs={{24,0},{32,8},{40,16},{48,24},{56,32},{64,40},{72,48},{80,56},{88,... | collective-permute-start | bytes 245768 | tf_op jit(solution)/shard_map/ppermute | solution.py:10
  47.9 21.2 %collective-permute-start.3 = (bf16[8,40,128]{2,1,0:T(8,128)(2,1)S(1)}, bf16[8,40,128]{2,1,0:T(8,128)(2,1)S(1)}, u32[]{:S(2)}, u32[]{:S(2)}) collective-permute-start(bf16[8,40,128]{2,1,0:T(8,128)(2,1)S(1)} %broadcast_select_fusion.2), channel_id=1, source_target_pairs={{0,8},{8,16},{16,24},{24,32},{32,40},{40,48},{48,56},{56,64},{64,7... | collective-permute-start | bytes 245768 | tf_op jit(solution)/shard_map/ppermute | solution.py:10
  52.8 16.3 %collective-permute-start.4 = (bf16[8,40,128]{2,1,0:T(8,128)(2,1)}, bf16[8,40,128]{2,1,0:T(8,128)(2,1)}, u32[]{:S(2)}, u32[]{:S(2)}) collective-permute-start(bf16[8,40,128]{2,1,0:T(8,128)(2,1)} %broadcast_select_fusion.1), channel_id=1, source_target_pairs={{0,16},{8,24},{16,32},{24,40},{32,48},{40,56},{48,64},{56,72},{64,... | collective-permute-start | bytes 245768 | tf_op jit(solution)/shard_map/ppermute | solution.py:10
  65.0 6.3 %collective-permute-start.5 = (bf16[8,40,128]{2,1,0:T(8,128)(2,1)S(1)}, bf16[8,40,128]{2,1,0:T(8,128)(2,1)S(1)}, u32[]{:S(2)}, u32[]{:S(2)}) collective-permute-start(bf16[8,40,128]{2,1,0:T(8,128)(2,1)S(1)} %broadcast_select_fusion), channel_id=1, source_target_pairs={{0,24},{8,32},{16,40},{24,48},{32,56},{40,64},{48,72},{56,80},{64,... | collective-permute-start | bytes 245768 | tf_op jit(solution)/shard_map/ppermute | solution.py:10
  72.1 4.2 %copy-start.1 = (bf16[1,6,40,128]{3,2,1,0:T(8,128)(2,1)S(1)}, bf16[1,6,40,128]{3,2,1,0:T(8,128)(2,1)}, u32[]{:S(2)}) copy-start(bf16[1,6,40,128]{3,2,1,0:T(8,128)(2,1)} %param.8) | copy-start | bytes 184324
Sparse Core Ops, SparseCore 0:
  79.2 284.9 all-reduce.2
where the time goes:
time: 374 us; the launch traced here: 372 us
  waiting for transfers between devices  286 us (76%)
  blocking collectives  27 us (7%)
  starting transfers between devices  23.3 us (6%)
  between operations  13.7 us (4%)
  local copies, waits for them, and re-layouts  9.76 us (3%)
  other arithmetic  9.31 us (2%)
    unnamed x2, waiting for transfers between devices  285 us
    all_gather x1, blocking collectives, shards(): subdomain_panel = lax.all_gather(deflation[0], 'grp', axis=0, tiled=True)  27 us
    ppermute x6, starting transfers between devices, shifted(): lax.ppermute(value, axis, [(source, source + steps) for source in range(l...  23.3 us
  transfers between devices with their start and end apart: 7, of which 2 were waited for; matrix products, arithmetic and copies ran while one was open for 3% of the time, Pallas kernels for 0%

commit v1 on v0

v1 whole, which is shorter than its diff:
```python
import functools

import jax
import jax.numpy as jnp
from jax import lax
from jax.experimental import pallas as pl
from jax.experimental.pallas import tpu as pltpu
from jax.sharding import PartitionSpec as P

OFFSETS = (1, 2, 3, -1, -2, -3)
ORDER = (2, 5, 1, 4, 0, 3)
SEND_COUNT = 8
MESH = pl.DeviceIdType.MESH


def kernel(
    sizes,
    defl,
    tiles,
    cols,
    neigh,
    lists,
    owner,
    out,
    panel,
    op,
    y_buf,
    z_buf,
    send_buf,
    recv_buf,
    g_buf,
    g_full,
    part_out,
    part_in,
    row_in,
    pick_out,
    pick_in,
    s_cols,
    s_neigh,
    s_lists,
    s_owner,
    load_sem,
    op_sem,
    table_sem,
    ring_send,
    ring_recv,
    margin_send,
    margin_recv,
    part_send,
    part_recv,
    row_send,
    row_recv,
    pick_send,
    pick_recv,
):
    subs, grps, wide, tall, blocks, width, nt = sizes
    lanes = 128
    own_blocks = blocks * grps
    total_cols = own_blocks + 6 * SEND_COUNT
    n_tiles = blocks * nt
    rows = width // grps
    half = grps // 2
    cut = blocks // 2

    i = lax.axis_index("sub")
    g = lax.axis_index("grp")
    row, col = i // wide, i % wide

    def grp_peer(step):
        return lax.rem(g + step + grps, grps)

    op_copies = [
        pltpu.make_async_copy(tiles.at[0, b], op.at[b], op_sem.at[b]) for b in range(blocks)
    ]
    table_copies = [
        pltpu.make_async_copy(cols, s_cols, table_sem.at[0]),
        pltpu.make_async_copy(neigh, s_neigh, table_sem.at[1]),
        pltpu.make_async_copy(lists, s_lists, table_sem.at[2]),
        pltpu.make_async_copy(owner, s_owner, table_sem.at[3]),
    ]
    own_copy = pltpu.make_async_copy(defl.at[0], panel.at[pl.ds(g * blocks, blocks)], load_sem)
    own_copy.start()
    for copy in op_copies + table_copies:
        copy.start()

    barrier = pltpu.get_barrier_semaphore()
    for step in range(1, grps):
        pl.semaphore_signal(barrier, inc=1, device_id=(i, grp_peer(step)), device_id_type=MESH)
    for step in range(1, wide):
        other = row * wide + lax.rem(col + step, wide)
        pl.semaphore_signal(barrier, inc=1, device_id=(other, g), device_id_type=MESH)
    for step in range(1, tall):
        other = lax.rem(row + step, tall) * wide + col
        pl.semaphore_signal(barrier, inc=1, device_id=(other, g), device_id_type=MESH)
    expected = grps + wide + tall - 3
    for off in OFFSETS:
        there = i + off
        valid = (there >= 0) & (there < subs)

        @pl.when(valid)
        def _():
            pl.semaphore_signal(barrier, inc=1, device_id=(there, g), device_id_type=MESH)

        expected = expected + valid.astype(jnp.int32)
    pl.semaphore_wait(barrier, expected)

    def ring(direction, step, piece):
        sign = 1 if direction == 0 else -1
        origin = grp_peer(-sign * step)
        place = panel.at[pl.ds(origin * blocks + piece * cut, cut)]
        source = defl.at[0, pl.ds(piece * cut, cut)] if step == 0 else place
        return pltpu.make_async_remote_copy(
            src_ref=source,
            dst_ref=place,
            send_sem=ring_send.at[direction, step, piece],
            recv_sem=ring_recv.at[direction, step, piece],
            device_id=(i, grp_peer(sign)),
            device_id_type=MESH,
        )

    def arriving(direction, step, piece):
        sign = 1 if direction == 0 else -1
        origin = grp_peer(-sign * (step + 1))
        place = panel.at[pl.ds(origin * blocks + piece * cut, cut)]
        return pltpu.make_async_remote_copy(
            src_ref=place,
            dst_ref=place,
            send_sem=ring_send.at[direction, step, piece],
            recv_sem=ring_recv.at[direction, step, piece],
            device_id=(i, grp_peer(sign)),
            device_id_type=MESH,
        )

    def travels(direction, step, piece):
        return step < half - 1 or (step == half - 1 and piece == direction)

    for piece in range(2):
        for direction in range(2):
            if travels(direction, 0, piece):
                ring(direction, 0, piece).start()

    def ring_step(step):
        for piece in range(2):
            for direction in range(2):
                if travels(direction, step, piece):
                    arriving(direction, step, piece).wait_recv()
                    if step + 1 < half and travels(direction, step + 1, piece):
                        ring(direction, step + 1, piece).start()

    def products(b):
        op_copies[b].wait()
        mine = panel[g * blocks + b]
        for t in range(nt):
            y_buf[pl.ds((b * nt + t) * width, width), :] = jnp.dot(
                mine, op[b, t], preferred_element_type=jnp.float32
            )

    def by_column(first, last, picker):
        for a in range(first, last):
            mine = y_buf[pl.ds(a, n_tiles, stride=width), :].astype(jnp.bfloat16)
            z_buf[pl.ds(a, total_cols, stride=width), :] = jnp.dot(
                picker, mine, preferred_element_type=jnp.float32
            )

    own_copy.wait()
    per_step = -(-blocks // max(1, half - 1))
    done = 0
    for step in range(half - 1):
        for b in range(done, min(blocks, done + per_step)):
            products(b)
        done = min(blocks, done + per_step)
        ring_step(step)
    for b in range(done, blocks):
        products(b)
    for copy in table_copies:
        copy.wait()
    lane_of = lax.broadcasted_iota(jnp.int32, (8, lanes), 1)
    named = jnp.full((8, lanes), -1, jnp.int32)
    for b in range(blocks):
        for t in range(nt):
            named = jnp.where(lane_of == b * nt + t, s_cols[b, 0, t], named)
    moved = named
    for r in range(6):
        low = own_blocks + r * SEND_COUNT
        within = (named >= low) & (named < low + SEND_COUNT)
        moved = moved + jnp.where(within, (s_neigh[0, r] - r) * SEND_COUNT, 0)
    named = jnp.broadcast_to(moved[0:1, :], (total_cols, lanes))
    hits = lax.broadcasted_iota(jnp.int32, (total_cols, lanes), 0) == named
    picker = jnp.where(hits, 1.0, 0.0).astype(jnp.bfloat16)[:, :n_tiles]
    ring_step(half - 1)

    def margin(o):
        there = i - OFFSETS[o]
        return pltpu.make_async_remote_copy(
            src_ref=send_buf.at[o],
            dst_ref=recv_buf.at[o],
            send_sem=margin_send.at[o],
            recv_sem=margin_recv.at[o],
            device_id=(there, g),
            device_id_type=MESH,
        )

    def inside(there):
        return (there >= 0) & (there < subs)

    for o in ORDER:
        for n in range(SEND_COUNT):
            send_buf[o, n] = panel[s_lists[o, 0, n]]

        @pl.when(inside(i - OFFSETS[o]))
        def _():
            margin(o).start()

    by_column(0, width, picker)

    def contract(first, count, blocks_of):
        left = [
            z_buf[pl.ds((first + n) * width, width), :].astype(jnp.bfloat16)
            for n in range(count)
        ]
        return lax.dot_general(
            jnp.concatenate(left, axis=1),
            jnp.concatenate(blocks_of, axis=1),
            (((1,), (1,)), ((), ())),
            preferred_element_type=jnp.float32,
        )

    g_buf[...] = jnp.zeros_like(g_buf)
    part_out[...] = jnp.zeros_like(part_out)
    g_full[...] = jnp.zeros_like(g_full)
    own = jnp.zeros((width, width), jnp.float32)
    for origin in range(grps):
        own = own + contract(origin * blocks, blocks, [panel[origin * blocks + b] for b in range(blocks)])
    g_full[:, pl.ds(0, width)] = own

    chosen = []
    for target in range(tall):
        place = jnp.int32(0)
        for c in range(1, wide):
            place = jnp.where(s_owner[row * wide + c] == target * wide + col, c, place)
        chosen.append(place)
    origin_row = jnp.int32(0)
    for s in range(subs):
        origin_row = jnp.where(s_owner[s] == i, s // wide, origin_row)

    for o in ORDER:

        @pl.when(inside(i + OFFSETS[o]))
        def _():
            margin(o).wait_recv()
            first = own_blocks + o * SEND_COUNT
            g_buf[o] = contract(first, SEND_COUNT, [recv_buf[o, n] for n in range(SEND_COUNT)])

    for r in range(6):
        slot = s_neigh[0, r]
        value = g_buf[jnp.maximum(slot, 0)]
        g_full[:, pl.ds((r + 1) * width, width)] = jnp.where(
            jnp.full((width, width), slot) >= 0, value, 0.0
        )

    spans = -(-7 * width // lanes)
    for other in range(grps):
        for span in range(spans):
            part_out[other, pl.ds(span * rows, rows), :] = g_full[
                pl.ds(other * rows, rows), pl.ds(span * lanes, lanes)
            ]

    def part(step):
        return pltpu.make_async_remote_copy(
            src_ref=part_out.at[grp_peer(step)],
            dst_ref=part_in.at[step],
            send_sem=part_send.at[step],
            recv_sem=part_recv.at[step],
            device_id=(i, grp_peer(step)),
            device_id_type=MESH,
        )

    near_first = sorted(range(1, grps), key=lambda s: -min(s, grps - s))
    for step in near_first:
        part(step).start()
    summed = part_out[g]
    for step in reversed(near_first):
        part(step).wait_recv()
        summed = summed + part_in[step]

    row_in[0] = summed

    def across(step):
        return pltpu.make_async_remote_copy(
            src_ref=row_in.at[0],
            dst_ref=row_in.at[step],
            send_sem=row_send.at[step],
            recv_sem=row_recv.at[step],
            device_id=(row * wide + lax.rem(col + step, wide), g),
            device_id_type=MESH,
        )

    for step in range(1, wide):
        across(step).start()
    for step in range(1, wide):
        across(step).wait_recv()
    for target in range(tall):
        pick_out[target] = row_in[lax.rem(col - chosen[target] + wide, wide)]

    def along(step):
        return pltpu.make_async_remote_copy(
            src_ref=pick_out.at[lax.rem(row + step, tall)],
            dst_ref=pick_in.at[step],
            send_sem=pick_send.at[step],
            recv_sem=pick_recv.at[step],
            device_id=(lax.rem(row + step, tall) * wide + col, g),
            device_id_type=MESH,
        )

    for step in range(1, tall):
        along(step).start()
    pick_in[0] = pick_out[row]
    for step in range(1, tall):
        along(step).wait_recv()
    final = pick_in[lax.rem(row - origin_row + tall, tall)]
    for span in range(spans):
        count = min(lanes, 7 * width - span * lanes)
        out[:, 0, pl.ds(span * lanes, count)] = final[span * rows : (span + 1) * rows, :count]

    for step in range(half):
        for piece in range(2):
            for direction in range(2):
                if travels(direction, step, piece):
                    ring(direction, step, piece).wait_send()
    for o in ORDER:

        @pl.when(inside(i - OFFSETS[o]))
        def _():
            margin(o).wait_send()

    for step in range(1, grps):
        part(step).wait_send()
    for step in range(1, wide):
        across(step).wait_send()
    for step in range(1, tall):
        along(step).wait_send()


def shards(deflation, operator_tiles, tile_columns, neighbours, send_blocks, row_owner):
    subs, grps = lax.axis_size("sub"), lax.axis_size("grp")
    wide = 1 << (subs.bit_length() // 2)
    tall = subs // wide
    _, blocks, width, lanes = deflation.shape
    nt = operator_tiles.shape[2]
    own_blocks = blocks * grps
    total_cols = own_blocks + 6 * SEND_COUNT
    spans = -(-7 * width // lanes)
    rows = width // grps
    packed = -(-spans * rows // 8) * 8
    bf16, f32, i32 = jnp.bfloat16, jnp.float32, jnp.int32
    dma = pltpu.SemaphoreType.DMA
    sizes = (subs, grps, wide, tall, blocks, width, nt)
    result = pl.pallas_call(
        functools.partial(kernel, sizes),
        out_shape=jax.ShapeDtypeStruct((rows, 1, 7 * width), f32),
        in_specs=[pl.BlockSpec(memory_space=pltpu.HBM)] * 6,
        out_specs=pl.BlockSpec(memory_space=pltpu.VMEM),
        scratch_shapes=[
            pltpu.VMEM((own_blocks, width, lanes), bf16),
            pltpu.VMEM((blocks, nt, lanes, lanes), bf16),
            pltpu.VMEM((blocks * nt * width, lanes), f32),
            pltpu.VMEM((total_cols * width, lanes), f32),
            pltpu.VMEM((6, SEND_COUNT, width, lanes), bf16),
            pltpu.VMEM((6, SEND_COUNT, width, lanes), bf16),
            pltpu.VMEM((6, width, width), f32),
            pltpu.VMEM((width, spans * lanes), f32),
            pltpu.VMEM((grps, packed, lanes), f32),
            pltpu.VMEM((grps, packed, lanes), f32),
            pltpu.VMEM((wide, packed, lanes), f32),
            pltpu.VMEM((tall, packed, lanes), f32),
            pltpu.VMEM((tall, packed, lanes), f32),
            pltpu.SMEM((blocks, 1, nt), i32),
            pltpu.SMEM((1, 6), i32),
            pltpu.SMEM((6, 1, SEND_COUNT), i32),
            pltpu.SMEM((subs,), i32),
            dma,
            dma((blocks,)),
            dma((4,)),
            dma((2, grps // 2, 2)),
            dma((2, grps // 2, 2)),
            dma((6,)),
            dma((6,)),
            dma((grps,)),
            dma((grps,)),
            dma((wide,)),
            dma((wide,)),
            dma((tall,)),
            dma((tall,)),
        ],
        compiler_params=pltpu.CompilerParams(
            collective_id=0, has_side_effects=True, vmem_limit_bytes=60 * 2**20
        ),
    )(
        deflation,
        operator_tiles,
        tile_columns.reshape(blocks, 1, nt),
        neighbours,
        send_blocks.reshape(6, 1, SEND_COUNT),
        row_owner,
    )
    return result.reshape(1, rows, 7 * width)


def solution(mesh):
    placed = (
        P("sub", "grp", None, None),
        P("sub", "grp", None, None, None),
        P("sub", "grp", None),
        P("sub", None),
        P("sub", None, None),
        P(),
    )
    return jax.shard_map(
        shards, mesh=mesh, in_specs=placed, out_specs=P("sub", "grp", None), check_vma=False
    )
```

time: 374 us -> 50.5 us (0.14)
  waiting for transfers between devices: 286 us -> 0 us
  Pallas kernels: 0 us -> 49 us
  blocking collectives: 27 us -> 0 us
  starting transfers between devices: 23.3 us -> 0 us
  between operations: 13.7 us -> 0.01 us
  other arithmetic: 9.31 us -> 0 us
  local copies, waits for them, and re-layouts: 9.76 us -> 1.29 us
    unnamed x2 -> x0, waiting for transfers between devices: 285 us -> none
    pallas_call x0 -> x1, Pallas kernels: none -> 49 us  [shards(): pl.pallas_call(functools.partial(kernel, sizes), out_shape=jax.ShapeDtype...]
    all_gather x1 -> x0, blocking collectives: 27 us -> none  [shards(): subdomain_panel = lax.all_gather(deflation[0], 'grp', axis=0, tiled=True)]
    ppermute x6 -> x0, starting transfers between devices: 23.3 us -> none  [shifted(): lax.ppermute(value, axis, [(source, source + steps) for source in range(l...]
    select_n x11 -> x0, other arithmetic: 5.64 us -> none  [the longest x1 2.3 us: shards(): jnp.where(jnp.arange(count_sub)[:, None, None] == target, galerkin[None],...]
    gather x8 -> x0, local copies, waits for them, and re-layouts: 5.5 us -> none  [the longest x6 3.41 us: shards(): chosen = jnp.take(subdomain_panel, send_blocks[0, slot_pos], axis=0)]
  transfers between devices with their start and end apart: 7 -> 0, of which waited for: 2 -> 0; matrix products, arithmetic and copies ran while one was open for 3% -> 0% of each run, Pallas kernels for 0% -> 0%
where the time goes in v1:
time: 50.5 us; the launch traced here: 50.3 us
  Pallas kernels  49 us (97%)
  local copies, waits for them, and re-layouts  1.29 us (3%)
    pallas_call x1, Pallas kernels, shards(): pl.pallas_call(functools.partial(kernel, sizes), out_shape=jax.ShapeDtype...  49 us
    unnamed x1, local copies, waits for them, and re-layouts  1.29 us

profile of v1, /device:TPU:1, one launch (start us, length us, event | category | flops | bytes accessed | tf_op | source)
XLA Modules:
  0.0 50.3 jit_solution(9502006314568634229)
XLA Ops:
  0.0 49.0 %shard_map.64 = f32[5,1,280]{2,1,0:T(1,128)} custom-call(bf16[1,6,40,128]{3,2,1,0:T(8,128)(2,1)} %defl.1, bf16[1,6,9,128,128]{4,3,2,1,0:T(8,128)(2,1)} %tiles.1, s32[6,1,9]{2,1,0:T(1,128)} %bitcast.4, s32[1,6]{1,0:T(1,128)} %neigh.1, s32[6,1,8]{2,1,0:T(1,128)} %bitcast.5, s32[64]{0:T(128)} %owner.1), custom_call_target="tpu_custom_call" | custom-call | tf_op jit(solution)/shard_map/pallas_call | solution.py:358
  49.0 1.3 %copy.8 = f32[1,5,280]{2,0,1:T(1,128)} copy(f32[1,5,280]{2,0,1:T(1,128)} %bitcast.3) | data formatting | bytes 11200

commit v2 on v1

--- a/solution.py
+++ b/solution.py
@@ -22,10 +22,17 @@
     lists,
     owner,
     out,
-    panel,
+    mine,
+    split,
+    half_panel,
+    spread,
     op,
     y_buf,
     z_buf,
+    z_split,
+    z_own,
+    z_margin,
+    z_sum,
     send_buf,
     recv_buf,
     g_buf,
@@ -42,8 +49,10 @@
     load_sem,
     op_sem,
     table_sem,
-    ring_send,
-    ring_recv,
+    panel_send,
+    panel_recv,
+    z_send,
+    z_recv,
     margin_send,
     margin_recv,
     part_send,
@@ -59,12 +68,14 @@
     total_cols = own_blocks + 6 * SEND_COUNT
     n_tiles = blocks * nt
     rows = width // grps
-    half = grps // 2
-    cut = blocks // 2
+    pairs = blocks // 2
+    own_pairs = own_blocks // 2
+    margin_pairs = SEND_COUNT // 2
 
     i = lax.axis_index("sub")
     g = lax.axis_index("grp")
     row, col = i // wide, i % wide
+    parity = lax.rem(g, 2)
 
     def grp_peer(step):
         return lax.rem(g + step + grps, grps)
@@ -78,10 +89,19 @@
         pltpu.make_async_copy(lists, s_lists, table_sem.at[2]),
         pltpu.make_async_copy(owner, s_owner, table_sem.at[3]),
     ]
-    own_copy = pltpu.make_async_copy(defl.at[0], panel.at[pl.ds(g * blocks, blocks)], load_sem)
+    own_copy = pltpu.make_async_copy(defl.at[0], mine, load_sem)
     own_copy.start()
     for copy in op_copies + table_copies:
         copy.start()
+
+    low_lanes = lax.broadcasted_iota(jnp.int32, (width, lanes), 1) < lanes // 2
+
+    def halves(first, second):
+        turned_first = pltpu.roll(first, lanes // 2, 1)
+        turned_second = pltpu.roll(second, lanes // 2, 1)
+        low = jnp.where(low_lanes, first, turned_second)
+        high = jnp.where(low_lanes, turned_first, second)
+        return low.astype(jnp.bfloat16), high.astype(jnp.bfloat16)
 
     barrier = pltpu.get_barrier_semaphore()
     for step in range(1, grps):
@@ -102,75 +122,53 @@
             pl.semaphore_signal(barrier, inc=1, device_id=(there, g), device_id_type=MESH)
 
         expected = expected + valid.astype(jnp.int32)
+    own_copy.wait()
+    for p in range(pairs):
+        first, second = mine[2 * p].astype(jnp.float32), mine[2 * p + 1].astype(jnp.float32)
+        split[0, p], split[1, p] = halves(first, second)
     pl.semaphore_wait(barrier, expected)
 
-    def ring(direction, step, piece):
-        sign = 1 if direction == 0 else -1
-        origin = grp_peer(-sign * step)
-        place = panel.at[pl.ds(origin * blocks + piece * cut, cut)]
-        source = defl.at[0, pl.ds(piece * cut, cut)] if step == 0 else place
-        return pltpu.make_async_remote_copy(
-            src_ref=source,
-            dst_ref=place,
-            send_sem=ring_send.at[direction, step, piece],
-            recv_sem=ring_recv.at[direction, step, piece],
-            device_id=(i, grp_peer(sign)),
-            device_id_type=MESH,
-        )
-
-    def arriving(direction, step, piece):
-        sign = 1 if direction == 0 else -1
-        origin = grp_peer(-sign * (step + 1))
-        place = panel.at[pl.ds(origin * blocks + piece * cut, cut)]
+    def panel_copy(step):
+        return pltpu.make_async_remote_copy(
+            src_ref=split.at[lax.rem(g + step, 2)],
+            dst_ref=half_panel.at[pl.ds(g * pairs, pairs)],
+            send_sem=panel_send.at[step],
+            recv_sem=panel_recv.at[step],
+            device_id=(i, grp_peer(step)),
+            device_id_type=MESH,
+        )
+
+    def panel_arrival(step):
+        place = half_panel.at[pl.ds(grp_peer(-step) * pairs, pairs)]
         return pltpu.make_async_remote_copy(
             src_ref=place,
             dst_ref=place,
-            send_sem=ring_send.at[direction, step, piece],
-            recv_sem=ring_recv.at[direction, step, piece],
-            device_id=(i, grp_peer(sign)),
-            device_id_type=MESH,
-        )
-
-    def travels(direction, step, piece):
-        return step < half - 1 or (step == half - 1 and piece == direction)
-
-    for piece in range(2):
-        for direction in range(2):
-            if travels(direction, 0, piece):
-                ring(direction, 0, piece).start()
-
-    def ring_step(step):
-        for piece in range(2):
-            for direction in range(2):
-                if travels(direction, step, piece):
-                    arriving(direction, step, piece).wait_recv()
-                    if step + 1 < half and travels(direction, step + 1, piece):
-                        ring(direction, step + 1, piece).start()
+            send_sem=panel_send.at[step],
+            recv_sem=panel_recv.at[step],
+            device_id=(i, grp_peer(step)),
+            device_id_type=MESH,
+        )
+
+    near_first = sorted(range(1, grps), key=lambda s: min(s, grps - s))
+    for step in reversed(near_first):
+        panel_copy(step).start()
 
     def products(b):
         op_copies[b].wait()
-        mine = panel[g * blocks + b]
+        left = mine[b]
         for t in range(nt):
             y_buf[pl.ds((b * nt + t) * width, width), :] = jnp.dot(
-                mine, op[b, t], preferred_element_type=jnp.float32
+                left, op[b, t], preferred_element_type=jnp.float32
             )
 
     def by_column(first, last, picker):
         for a in range(first, last):
-            mine = y_buf[pl.ds(a, n_tiles, stride=width), :].astype(jnp.bfloat16)
+            by_tile = y_buf[pl.ds(a, n_tiles, stride=width), :].astype(jnp.bfloat16)
             z_buf[pl.ds(a, total_cols, stride=width), :] = jnp.dot(
-                picker, mine, preferred_element_type=jnp.float32
+                picker, by_tile, preferred_element_type=jnp.float32
             )
 
-    own_copy.wait()
-    per_step = -(-blocks // max(1, half - 1))
-    done = 0
-    for step in range(half - 1):
-        for b in range(done, min(blocks, done + per_step)):
-            products(b)
-        done = min(blocks, done + per_step)
-        ring_step(step)
-    for b in range(done, blocks):
+    for b in range(blocks):
         products(b)
     for copy in table_copies:
         copy.wait()
@@ -187,7 +185,39 @@
     named = jnp.broadcast_to(moved[0:1, :], (total_cols, lanes))
     hits = lax.broadcasted_iota(jnp.int32, (total_cols, lanes), 0) == named
     picker = jnp.where(hits, 1.0, 0.0).astype(jnp.bfloat16)[:, :n_tiles]
-    ring_step(half - 1)
+    by_column(0, width, picker)
+    for p in range(total_cols // 2):
+        first = z_buf[pl.ds(2 * p * width, width), :]
+        second = z_buf[pl.ds((2 * p + 1) * width, width), :]
+        z_split[0, p], z_split[1, p] = halves(first, second)
+
+    def z_copy(which):
+        first, count = (0, own_pairs) if which == 0 else (own_pairs, 6 * margin_pairs)
+        return pltpu.make_async_remote_copy(
+            src_ref=z_split.at[1 - parity, pl.ds(first, count)],
+            dst_ref=(z_own, z_margin)[which],
+            send_sem=z_send.at[which],
+            recv_sem=z_recv.at[which],
+            device_id=(i, grp_peer(2 * which - 1)),
+            device_id_type=MESH,
+        )
+
+    z_copy(0).start()
+    z_copy(1).start()
+
+    def spread_blocks(origin):
+        for p in range(pairs):
+            packed = half_panel[origin * pairs + p].astype(jnp.float32)
+            turned = pltpu.roll(packed, lanes // 2, 1)
+            spread[origin * blocks + 2 * p] = jnp.where(low_lanes, packed, turned)
+            spread[origin * blocks + 2 * p + 1] = jnp.where(low_lanes, turned, packed)
+
+    for p in range(pairs):
+        half_panel[g * pairs + p] = split[parity, p]
+    spread_blocks(g)
+    for step in near_first:
+        panel_arrival(step).wait_recv()
+        spread_blocks(grp_peer(-step))
 
     def margin(o):
         there = i - OFFSETS[o]
@@ -204,23 +234,18 @@
         return (there >= 0) & (there < subs)
 
     for o in ORDER:
-        for n in range(SEND_COUNT):
-            send_buf[o, n] = panel[s_lists[o, 0, n]]
+        for p in range(margin_pairs):
+            first, second = spread[s_lists[o, 0, 2 * p]], spread[s_lists[o, 0, 2 * p + 1]]
+            send_buf[o, p] = jnp.where(low_lanes, first, second).astype(jnp.bfloat16)
 
         @pl.when(inside(i - OFFSETS[o]))
         def _():
             margin(o).start()
 
-    by_column(0, width, picker)
-
-    def contract(first, count, blocks_of):
-        left = [
-            z_buf[pl.ds((first + n) * width, width), :].astype(jnp.bfloat16)
-            for n in range(count)
-        ]
+    def contract(left, right):
         return lax.dot_general(
             jnp.concatenate(left, axis=1),
-            jnp.concatenate(blocks_of, axis=1),
+            jnp.concatenate(right, axis=1),
             (((1,), (1,)), ((), ())),
             preferred_element_type=jnp.float32,
         )
@@ -228,11 +253,6 @@
     g_buf[...] = jnp.zeros_like(g_buf)
     part_out[...] = jnp.zeros_like(part_out)
     g_full[...] = jnp.zeros_like(g_full)
-    own = jnp.zeros((width, width), jnp.float32)
-    for origin in range(grps):
-        own = own + contract(origin * blocks, blocks, [panel[origin * blocks + b] for b in range(blocks)])
-    g_full[:, pl.ds(0, width)] = own
-
     chosen = []
     for target in range(tall):
         place = jnp.int32(0)
@@ -243,13 +263,29 @@
     for s in range(subs):
         origin_row = jnp.where(s_owner[s] == i, s // wide, origin_row)
 
+    def both(theirs, p, q):
+        total = z_split[parity, p].astype(jnp.float32) + theirs[q].astype(jnp.float32)
+        return total.astype(jnp.bfloat16)
+
+    z_copy(0).wait_recv()
+    own = jnp.zeros((width, width), jnp.float32)
+    for origin in range(grps):
+        places = range(origin * pairs, (origin + 1) * pairs)
+        own = own + contract([both(z_own, p, p) for p in places], [half_panel[p] for p in places])
+    g_full[:, pl.ds(0, width)] = own
+    z_copy(1).wait_recv()
+    for p in range(6 * margin_pairs):
+        z_sum[p] = both(z_margin, own_pairs + p, p)
+
     for o in ORDER:
 
         @pl.when(inside(i + OFFSETS[o]))
         def _():
             margin(o).wait_recv()
-            first = own_blocks + o * SEND_COUNT
-            g_buf[o] = contract(first, SEND_COUNT, [recv_buf[o, n] for n in range(SEND_COUNT)])
+            places = range(margin_pairs)
+            g_buf[o] = contract(
+                [z_sum[o * margin_pairs + p] for p in places], [recv_buf[o, p] for p in places]
+            )
 
     for r in range(6):
         slot = s_neigh[0, r]
@@ -275,11 +311,10 @@
             device_id_type=MESH,
         )
 
-    near_first = sorted(range(1, grps), key=lambda s: -min(s, grps - s))
-    for step in near_first:
+    for step in reversed(near_first):
         part(step).start()
     summed = part_out[g]
-    for step in reversed(near_first):
+    for step in near_first:
         part(step).wait_recv()
         summed = summed + part_in[step]
 
@@ -322,11 +357,10 @@
         count = min(lanes, 7 * width - span * lanes)
         out[:, 0, pl.ds(span * lanes, count)] = final[span * rows : (span + 1) * rows, :count]
 
-    for step in range(half):
-        for piece in range(2):
-            for direction in range(2):
-                if travels(direction, step, piece):
-                    ring(direction, step, piece).wait_send()
+    for step in range(1, grps):
+        panel_copy(step).wait_send()
+    z_copy(0).wait_send()
+    z_copy(1).wait_send()
     for o in ORDER:
 
         @pl.when(inside(i - OFFSETS[o]))
@@ -361,12 +395,19 @@
         in_specs=[pl.BlockSpec(memory_space=pltpu.HBM)] * 6,
         out_specs=pl.BlockSpec(memory_space=pltpu.VMEM),
         scratch_shapes=[
-            pltpu.VMEM((own_blocks, width, lanes), bf16),
+            pltpu.VMEM((blocks, width, lanes), bf16),
+            pltpu.VMEM((2, blocks // 2, width, lanes), bf16),
+            pltpu.VMEM((own_blocks // 2, width, lanes), bf16),
+            pltpu.VMEM((own_blocks, width, lanes), f32),
             pltpu.VMEM((blocks, nt, lanes, lanes), bf16),
             pltpu.VMEM((blocks * nt * width, lanes), f32),
             pltpu.VMEM((total_cols * width, lanes), f32),
-            pltpu.VMEM((6, SEND_COUNT, width, lanes), bf16),
-            pltpu.VMEM((6, SEND_COUNT, width, lanes), bf16),
+            pltpu.VMEM((2, total_cols // 2, width, lanes), bf16),
+            pltpu.VMEM((own_blocks // 2, width, lanes), bf16),
+            pltpu.VMEM((3 * SEND_COUNT, width, lanes), bf16),
+            pltpu.VMEM((3 * SEND_COUNT, width, lanes), bf16),
+            pltpu.VMEM((6, SEND_COUNT // 2, width, lanes), bf16),
+            pltpu.VMEM((6, SEND_COUNT // 2, width, lanes), bf16),
             pltpu.VMEM((6, width, width), f32),
             pltpu.VMEM((width, spans * lanes), f32),
             pltpu.VMEM((grps, packed, lanes), f32),
@@ -381,8 +422,10 @@
             dma,
             dma((blocks,)),
             dma((4,)),
-            dma((2, grps // 2, 2)),
-            dma((2, grps // 2, 2)),
+            dma((grps,)),
+            dma((grps,)),
+            dma((2,)),
+            dma((2,)),
             dma((6,)),
             dma((6,)),
             dma((grps,)),

time: 50.5 us -> 45.8 us (0.907)
  Pallas kernels: 49 us -> 44.3 us
    pallas_call x1, Pallas kernels: 49 us -> 44.3 us  [shards(): pl.pallas_call(functools.partial(kernel, sizes), out_shape=jax.ShapeDtype...]
where the time goes in v2:
time: 45.8 us; the launch traced here: 45.6 us
  Pallas kernels  44.3 us (97%)
  local copies, waits for them, and re-layouts  1.29 us (3%)
    pallas_call x1, Pallas kernels, shards(): pl.pallas_call(functools.partial(kernel, sizes), out_shape=jax.ShapeDtype...  44.3 us
    unnamed x1, local copies, waits for them, and re-layouts  1.29 us

profile of v2, /device:TPU:1, one launch (start us, length us, event | category | flops | bytes accessed | tf_op | source)
XLA Modules:
  0.0 45.6 jit_solution(18306485736183472353)
XLA Ops:
  0.0 44.3 %shard_map.64 = f32[5,1,280]{2,1,0:T(1,128)} custom-call(bf16[1,6,40,128]{3,2,1,0:T(8,128)(2,1)} %defl.1, bf16[1,6,9,128,128]{4,3,2,1,0:T(8,128)(2,1)} %tiles.1, s32[6,1,9]{2,1,0:T(1,128)} %bitcast.4, s32[1,6]{1,0:T(1,128)} %neigh.1, s32[6,1,8]{2,1,0:T(1,128)} %bitcast.5, s32[64]{0:T(128)} %owner.1), custom_call_target="tpu_custom_call" | custom-call | tf_op jit(solution)/shard_map/pallas_call | solution.py:392
  44.3 1.3 %copy.8 = f32[1,5,280]{2,0,1:T(1,128)} copy(f32[1,5,280]{2,0,1:T(1,128)} %bitcast.3) | data formatting | bytes 11200

commit v3 on v2

--- a/solution.py
+++ b/solution.py
@@ -11,6 +11,10 @@
 ORDER = (2, 5, 1, 4, 0, 3)
 SEND_COUNT = 8
 MESH = pl.DeviceIdType.MESH
+
+
+def reaches_of(subs):
+    return [1 << level for level in range(1, max(1, subs.bit_length() - 2))]
 
 
 def kernel(
@@ -61,12 +65,14 @@
     row_recv,
     pick_send,
     pick_recv,
+    greet_sem,
 ):
     subs, grps, wide, tall, blocks, width, nt = sizes
     lanes = 128
     own_blocks = blocks * grps
     total_cols = own_blocks + 6 * SEND_COUNT
     n_tiles = blocks * nt
+    reaches = reaches_of(subs)
     rows = width // grps
     pairs = blocks // 2
     own_pairs = own_blocks // 2
@@ -79,6 +85,20 @@
 
     def grp_peer(step):
         return lax.rem(g + step + grps, grps)
+
+    def sub_peer(step):
+        return lax.rem(i + step + subs, subs)
+
+    def greet(level):
+        if level < len(reaches):
+            for step in (reaches[level], -reaches[level]):
+                pl.semaphore_signal(
+                    greet_sem.at[level], inc=1, device_id=(sub_peer(step), g), device_id_type=MESH
+                )
+
+    def greeted(level):
+        if level < len(reaches):
+            pl.semaphore_wait(greet_sem.at[level], 2)
 
     op_copies = [
         pltpu.make_async_copy(tiles.at[0, b], op.at[b], op_sem.at[b]) for b in range(blocks)
@@ -91,8 +111,6 @@
     ]
     own_copy = pltpu.make_async_copy(defl.at[0], mine, load_sem)
     own_copy.start()
-    for copy in op_copies + table_copies:
-        copy.start()
 
     low_lanes = lax.broadcasted_iota(jnp.int32, (width, lanes), 1) < lanes // 2
 
@@ -106,27 +124,13 @@
     barrier = pltpu.get_barrier_semaphore()
     for step in range(1, grps):
         pl.semaphore_signal(barrier, inc=1, device_id=(i, grp_peer(step)), device_id_type=MESH)
-    for step in range(1, wide):
-        other = row * wide + lax.rem(col + step, wide)
-        pl.semaphore_signal(barrier, inc=1, device_id=(other, g), device_id_type=MESH)
-    for step in range(1, tall):
-        other = lax.rem(row + step, tall) * wide + col
-        pl.semaphore_signal(barrier, inc=1, device_id=(other, g), device_id_type=MESH)
-    expected = grps + wide + tall - 3
-    for off in OFFSETS:
-        there = i + off
-        valid = (there >= 0) & (there < subs)
-
-        @pl.when(valid)
-        def _():
-            pl.semaphore_signal(barrier, inc=1, device_id=(there, g), device_id_type=MESH)
-
-        expected = expected + valid.astype(jnp.int32)
+    for step in (1, -1, 2, -2):
+        pl.semaphore_signal(barrier, inc=1, device_id=(sub_peer(step), g), device_id_type=MESH)
     own_copy.wait()
     for p in range(pairs):
         first, second = mine[2 * p].astype(jnp.float32), mine[2 * p + 1].astype(jnp.float32)
         split[0, p], split[1, p] = halves(first, second)
-    pl.semaphore_wait(barrier, expected)
+    pl.semaphore_wait(barrier, grps + 3)
 
     def panel_copy(step):
         return pltpu.make_async_remote_copy(
@@ -152,6 +156,9 @@
     near_first = sorted(range(1, grps), key=lambda s: min(s, grps - s))
     for step in reversed(near_first):
         panel_copy(step).start()
+    greet(0)
+    for copy in op_copies + table_copies:
+        copy.start()
 
     def products(b):
         op_copies[b].wait()
@@ -170,6 +177,8 @@
 
     for b in range(blocks):
         products(b)
+    greeted(0)
+    greet(1)
     for copy in table_copies:
         copy.wait()
     lane_of = lax.broadcasted_iota(jnp.int32, (8, lanes), 1)
@@ -204,6 +213,8 @@
 
     z_copy(0).start()
     z_copy(1).start()
+    greeted(1)
+    greet(2)
 
     def spread_blocks(origin):
         for p in range(pairs):
@@ -250,7 +261,14 @@
             preferred_element_type=jnp.float32,
         )
 
-    g_buf[...] = jnp.zeros_like(g_buf)
+    greeted(2)
+    greet(3)
+    for o in range(6):
+
+        @pl.when(jnp.logical_not(inside(i + OFFSETS[o])))
+        def _():
+            recv_buf[o] = jnp.zeros_like(recv_buf[o])
+
     part_out[...] = jnp.zeros_like(part_out)
     g_full[...] = jnp.zeros_like(g_full)
     chosen = []
@@ -282,10 +300,12 @@
         @pl.when(inside(i + OFFSETS[o]))
         def _():
             margin(o).wait_recv()
-            places = range(margin_pairs)
-            g_buf[o] = contract(
-                [z_sum[o * margin_pairs + p] for p in places], [recv_buf[o, p] for p in places]
-            )
+
+    places = range(margin_pairs)
+    for o in range(6):
+        g_buf[o] = contract(
+            [z_sum[o * margin_pairs + p] for p in places], [recv_buf[o, p] for p in places]
+        )
 
     for r in range(6):
         slot = s_neigh[0, r]
@@ -301,6 +321,8 @@
                 pl.ds(other * rows, rows), pl.ds(span * lanes, lanes)
             ]
 
+    greeted(3)
+
     def part(step):
         return pltpu.make_async_remote_copy(
             src_ref=part_out.at[grp_peer(step)],
@@ -313,6 +335,16 @@
 
     for step in reversed(near_first):
         part(step).start()
+    for step in range(1, grps):
+        panel_copy(step).wait_send()
+    z_copy(0).wait_send()
+    z_copy(1).wait_send()
+    for o in ORDER:
+
+        @pl.when(inside(i - OFFSETS[o]))
+        def _():
+            margin(o).wait_send()
+
     summed = part_out[g]
     for step in near_first:
         part(step).wait_recv()
@@ -332,6 +364,8 @@
 
     for step in range(1, wide):
         across(step).start()
+    for step in range(1, grps):
+        part(step).wait_send()
     for step in range(1, wide):
         across(step).wait_recv()
     for target in range(tall):
@@ -350,6 +384,8 @@
     for step in range(1, tall):
         along(step).start()
     pick_in[0] = pick_out[row]
+    for step in range(1, wide):
+        across(step).wait_send()
     for step in range(1, tall):
         along(step).wait_recv()
     final = pick_in[lax.rem(row - origin_row + tall, tall)]
@@ -357,20 +393,6 @@
         count = min(lanes, 7 * width - span * lanes)
         out[:, 0, pl.ds(span * lanes, count)] = final[span * rows : (span + 1) * rows, :count]
 
-    for step in range(1, grps):
-        panel_copy(step).wait_send()
-    z_copy(0).wait_send()
-    z_copy(1).wait_send()
-    for o in ORDER:
-
-        @pl.when(inside(i - OFFSETS[o]))
-        def _():
-            margin(o).wait_send()
-
-    for step in range(1, grps):
-        part(step).wait_send()
-    for step in range(1, wide):
-        across(step).wait_send()
     for step in range(1, tall):
         along(step).wait_send()
 
@@ -434,6 +456,7 @@
             dma((wide,)),
             dma((tall,)),
             dma((tall,)),
+            pltpu.SemaphoreType.REGULAR((max(1, len(reaches_of(subs))),)),
         ],
         compiler_params=pltpu.CompilerParams(
             collective_id=0, has_side_effects=True, vmem_limit_bytes=60 * 2**20

time: 45.8 us -> 44.5 us (0.972)
  Pallas kernels: 44.3 us -> 43 us
    pallas_call x1, Pallas kernels: 44.3 us -> 43 us  [shards(): pl.pallas_call(functools.partial(kernel, sizes), out_shape=jax.ShapeDtype...]
where the time goes in v3:
time: 44.5 us; the launch traced here: 44.3 us
  Pallas kernels  43 us (97%)
  local copies, waits for them, and re-layouts  1.29 us (3%)
    pallas_call x1, Pallas kernels, shards(): pl.pallas_call(functools.partial(kernel, sizes), out_shape=jax.ShapeDtype...  43 us
    unnamed x1, local copies, waits for them, and re-layouts  1.29 us

profile of v3, /device:TPU:1, one launch (start us, length us, event | category | flops | bytes accessed | tf_op | source)
XLA Modules:
  0.0 44.3 jit_solution(16499264441106526996)
XLA Ops:
  0.0 43.0 %shard_map.64 = f32[5,1,280]{2,1,0:T(1,128)} custom-call(bf16[1,6,40,128]{3,2,1,0:T(8,128)(2,1)} %defl.1, bf16[1,6,9,128,128]{4,3,2,1,0:T(8,128)(2,1)} %tiles.1, s32[6,1,9]{2,1,0:T(1,128)} %bitcast.4, s32[1,6]{1,0:T(1,128)} %neigh.1, s32[6,1,8]{2,1,0:T(1,128)} %bitcast.5, s32[64]{0:T(128)} %owner.1), custom_call_target="tpu_custom_call" | custom-call | tf_op jit(solution)/shard_map/pallas_call | solution.py:414
  43.0 1.3 %copy.8 = f32[1,5,280]{2,0,1:T(1,128)} copy(f32[1,5,280]{2,0,1:T(1,128)} %bitcast.3) | data formatting | bytes 11200

commit v4 on v3

--- a/solution.py
+++ b/solution.py
@@ -459,15 +459,20 @@
             pltpu.SemaphoreType.REGULAR((max(1, len(reaches_of(subs))),)),
         ],
         compiler_params=pltpu.CompilerParams(
-            collective_id=0, has_side_effects=True, vmem_limit_bytes=60 * 2**20
+            collective_id=0, has_side_effects=True, vmem_limit_bytes=40 * 2**20
         ),
     )(
-        deflation,
-        operator_tiles,
-        tile_columns.reshape(blocks, 1, nt),
-        neighbours,
-        send_blocks.reshape(6, 1, SEND_COUNT),
-        row_owner,
+        *(
+            pltpu.with_memory_space_constraint(operand, pltpu.HBM)
+            for operand in (
+                deflation,
+                operator_tiles,
+                tile_columns.reshape(blocks, 1, nt),
+                neighbours,
+                send_blocks.reshape(6, 1, SEND_COUNT),
+                row_owner,
+            )
+        )
     )
     return result.reshape(1, rows, 7 * width)
 

time: 44.5 us -> 43.2 us (0.971)
  local copies, waits for them, and re-layouts: 1.29 us -> 0.6 us
  Pallas kernels: 43 us -> 42.4 us
    unnamed x1, local copies, waits for them, and re-layouts: 1.29 us -> 0.6 us
    pallas_call x1, Pallas kernels: 43 us -> 42.4 us  [shards(): pl.pallas_call(functools.partial(kernel, sizes), out_shape=jax.ShapeDtype...]
where the time goes in v4:
time: 43.2 us; the launch traced here: 43 us
  Pallas kernels  42.4 us (98%)
  local copies, waits for them, and re-layouts  0.6 us (1%)
    pallas_call x1, Pallas kernels, shards(): pl.pallas_call(functools.partial(kernel, sizes), out_shape=jax.ShapeDtype...  42.4 us

profile of v4, /device:TPU:1, one launch (start us, length us, event | category | flops | bytes accessed | tf_op | source)
XLA Modules:
  0.0 43.0 jit_solution(14227144256812799219)
XLA Ops:
  0.0 42.4 %shard_map.64 = f32[5,1,280]{2,1,0:T(1,128)S(1)} custom-call(bf16[1,6,40,128]{3,2,1,0:T(8,128)(2,1)} %defl.1, bf16[1,6,9,128,128]{4,3,2,1,0:T(8,128)(2,1)} %tiles.1, s32[6,1,9]{2,1,0:T(1,128)} %bitcast.4, s32[1,6]{1,0:T(1,128)} %neigh.1, s32[6,1,8]{2,1,0:T(1,128)} %bitcast.5, s32[64]{0:T(128)} %owner.1), custom_call_target="tpu_custom_call" | custom-call | tf_op jit(solution)/shard_map/pallas_call | solution.py:414
  42.4 0.6 %copy.8 = f32[1,5,280]{2,0,1:T(1,128)} copy(f32[1,5,280]{2,0,1:T(1,128)S(1)} %bitcast.3) | data formatting | bytes 11200

commit v5 on v4

--- a/solution.py
+++ b/solution.py
@@ -154,7 +154,7 @@
         )
 
     near_first = sorted(range(1, grps), key=lambda s: min(s, grps - s))
-    for step in reversed(near_first):
+    for step in near_first:
         panel_copy(step).start()
     greet(0)
     for copy in op_copies + table_copies:
@@ -244,6 +244,8 @@
     def inside(there):
         return (there >= 0) & (there < subs)
 
+    greeted(2)
+    greet(3)
     for o in ORDER:
         for p in range(margin_pairs):
             first, second = spread[s_lists[o, 0, 2 * p]], spread[s_lists[o, 0, 2 * p + 1]]
@@ -261,8 +263,6 @@
             preferred_element_type=jnp.float32,
         )
 
-    greeted(2)
-    greet(3)
     for o in range(6):
 
         @pl.when(jnp.logical_not(inside(i + OFFSETS[o])))
@@ -362,7 +362,7 @@
             device_id_type=MESH,
         )
 
-    for step in range(1, wide):
+    for step in sorted(range(1, wide), key=lambda s: -min(s, wide - s)):
         across(step).start()
     for step in range(1, grps):
         part(step).wait_send()
@@ -381,7 +381,7 @@
             device_id_type=MESH,
         )
 
-    for step in range(1, tall):
+    for step in sorted(range(1, tall), key=lambda s: -min(s, tall - s)):
         along(step).start()
     pick_in[0] = pick_out[row]
     for step in range(1, wide):

time: 43.2 us -> 42.8 us (level)
  no operation moved by 1% of the time
where the time goes in v5:
time: 42.8 us; the launch traced here: 42.6 us
  Pallas kernels  42 us (98%)
  local copies, waits for them, and re-layouts  0.6 us (1%)
    pallas_call x1, Pallas kernels, shards(): pl.pallas_call(functools.partial(kernel, sizes), out_shape=jax.ShapeDtype...  42 us

profile of v5, /device:TPU:1, one launch (start us, length us, event | category | flops | bytes accessed | tf_op | source)
XLA Modules:
  0.0 42.6 jit_solution(13668688512311127280)
XLA Ops:
  0.0 42.0 %shard_map.64 = f32[5,1,280]{2,1,0:T(1,128)S(1)} custom-call(bf16[1,6,40,128]{3,2,1,0:T(8,128)(2,1)} %defl.1, bf16[1,6,9,128,128]{4,3,2,1,0:T(8,128)(2,1)} %tiles.1, s32[6,1,9]{2,1,0:T(1,128)} %bitcast.4, s32[1,6]{1,0:T(1,128)} %neigh.1, s32[6,1,8]{2,1,0:T(1,128)} %bitcast.5, s32[64]{0:T(128)} %owner.1), custom_call_target="tpu_custom_call" | custom-call | tf_op jit(solution)/shard_map/pallas_call | solution.py:414
  42.0 0.6 %copy.8 = f32[1,5,280]{2,0,1:T(1,128)} copy(f32[1,5,280]{2,0,1:T(1,128)S(1)} %bitcast.3) | data formatting | bytes 11200

commit v6 on v5

--- a/solution.py
+++ b/solution.py
@@ -290,7 +290,7 @@
     for origin in range(grps):
         places = range(origin * pairs, (origin + 1) * pairs)
         own = own + contract([both(z_own, p, p) for p in places], [half_panel[p] for p in places])
-    g_full[:, pl.ds(0, width)] = own
+    g_full[pl.ds(0, width), pl.ds(0, width)] = own
     z_copy(1).wait_recv()
     for p in range(6 * margin_pairs):
         z_sum[p] = both(z_margin, own_pairs + p, p)
@@ -310,11 +310,12 @@
     for r in range(6):
         slot = s_neigh[0, r]
         value = g_buf[jnp.maximum(slot, 0)]
-        g_full[:, pl.ds((r + 1) * width, width)] = jnp.where(
+        g_full[pl.ds(0, width), pl.ds((r + 1) * width, width)] = jnp.where(
             jnp.full((width, width), slot) >= 0, value, 0.0
         )
 
     spans = -(-7 * width // lanes)
+    packed = part_in.shape[1]
     for other in range(grps):
         for span in range(spans):
             part_out[other, pl.ds(span * rows, rows), :] = g_full[
@@ -325,7 +326,7 @@
 
     def part(step):
         return pltpu.make_async_remote_copy(
-            src_ref=part_out.at[grp_peer(step)],
+            src_ref=part_out.at[grp_peer(step), pl.ds(0, packed)],
             dst_ref=part_in.at[step],
             send_sem=part_send.at[step],
             recv_sem=part_recv.at[step],
@@ -345,7 +346,7 @@
         def _():
             margin(o).wait_send()
 
-    summed = part_out[g]
+    summed = part_out[g, pl.ds(0, packed)]
     for step in near_first:
         part(step).wait_recv()
         summed = summed + part_in[step]
@@ -422,8 +423,8 @@
             pltpu.VMEM((own_blocks // 2, width, lanes), bf16),
             pltpu.VMEM((own_blocks, width, lanes), f32),
             pltpu.VMEM((blocks, nt, lanes, lanes), bf16),
-            pltpu.VMEM((blocks * nt * width, lanes), f32),
-            pltpu.VMEM((total_cols * width, lanes), f32),
+            pltpu.VMEM(((blocks * nt + 8) * width, lanes), f32),
+            pltpu.VMEM(((total_cols + 8) * width, lanes), f32),
             pltpu.VMEM((2, total_cols // 2, width, lanes), bf16),
             pltpu.VMEM((own_blocks // 2, width, lanes), bf16),
             pltpu.VMEM((3 * SEND_COUNT, width, lanes), bf16),
@@ -431,8 +432,8 @@
             pltpu.VMEM((6, SEND_COUNT // 2, width, lanes), bf16),
             pltpu.VMEM((6, SEND_COUNT // 2, width, lanes), bf16),
             pltpu.VMEM((6, width, width), f32),
-            pltpu.VMEM((width, spans * lanes), f32),
-            pltpu.VMEM((grps, packed, lanes), f32),
+            pltpu.VMEM((width + 8, spans * lanes), f32),
+            pltpu.VMEM((grps, packed + 8, lanes), f32),
             pltpu.VMEM((grps, packed, lanes), f32),
             pltpu.VMEM((wide, packed, lanes), f32),
             pltpu.VMEM((tall, packed, lanes), f32),

time: 42.8 us -> 42.8 us (level)
  no operation moved by 1% of the time
where the time goes in v6:
time: 42.8 us; the launch traced here: 42.6 us
  Pallas kernels  42 us (98%)
  local copies, waits for them, and re-layouts  0.6 us (1%)
    pallas_call x1, Pallas kernels, shards(): pl.pallas_call(functools.partial(kernel, sizes), out_shape=jax.ShapeDtype...  42 us

profile of v6, /device:TPU:1, one launch (start us, length us, event | category | flops | bytes accessed | tf_op | source)
XLA Modules:
  0.0 42.6 jit_solution(167822763216342223)
XLA Ops:
  0.0 42.0 %shard_map.64 = f32[5,1,280]{2,1,0:T(1,128)S(1)} custom-call(bf16[1,6,40,128]{3,2,1,0:T(8,128)(2,1)} %defl.1, bf16[1,6,9,128,128]{4,3,2,1,0:T(8,128)(2,1)} %tiles.1, s32[6,1,9]{2,1,0:T(1,128)} %bitcast.4, s32[1,6]{1,0:T(1,128)} %neigh.1, s32[6,1,8]{2,1,0:T(1,128)} %bitcast.5, s32[64]{0:T(128)} %owner.1), custom_call_target="tpu_custom_call" | custom-call | tf_op jit(solution)/shard_map/pallas_call | solution.py:415
  42.0 0.6 %copy.8 = f32[1,5,280]{2,0,1:T(1,128)} copy(f32[1,5,280]{2,0,1:T(1,128)S(1)} %bitcast.3) | data formatting | bytes 11200
